TPU v7x, 256 devices: a whole 4x4x8 slice. The times are simulated.
256 devices in a mesh: ctx: 16 (over x_hi, z), head: 16 (over x_lo, y, core).
Axes of the slice: x: 4 (x_hi: 2, x_lo: 2; x = x_hi * 2 + x_lo), y: 4, z: 8, core: 2. Of those that a mesh axis runs over, the one named last changes fastest.
Arguments:
- hidden_in: bfloat16 [2048, 4096], P('ctx'), may hold values from -30 to 30
- query_weight: bfloat16 [4096, 8192], P(None, 'head'), may hold values from -0.1875 to 0.1875
- shared_weight: bfloat16 [4096, 512], P(None, 'head'), may hold values from -0.09375 to 0.09375
- out_weight: bfloat16 [8192, 4096], P('head'), may hold values from -1 to 1
- residual: bfloat16 [2048, 4096], P(('ctx', 'head')), may hold values from -20 to 20
- norm_gain: float32 [4096], replicated, may hold values from 0.25 to 1.75
Outputs:
- residual_out: bfloat16 [2048, 4096], P(('ctx', 'head'))
- normed: bfloat16 [2048, 4096], P('ctx')
All inputs are finite; a program needn't handle non-finite values.
Results may differ from a plain program's by a relative error of at most 0.0065.
The roundings to bfloat16 on the way count: a program that leaves them out, or rounds other values in their place, can miss the bound.
Values may be sent and summed in bfloat16 or wider, within the bound.
A program may use at most 64 MiB of HBM per device.

v0:
```python
import jax
import jax.numpy as jnp
from jax import lax
from jax.sharding import PartitionSpec as P

HD = 128
W1 = 512
W2 = 32


def from_behind(value, axis, steps):
    count = lax.axis_size(axis)
    initial, last = (max(0, -steps), min(count, count - steps))
    return lax.ppermute(value, axis, [(source, source + steps) for source in range(initial, last)])


def window_mask(first, rows, spread, reach):
    query_pos = first + jnp.arange(rows, dtype=jnp.int32)[:, None, None]
    offset = jnp.arange(spread, dtype=jnp.int32)[None, :, None]
    column = jnp.arange(rows + reach, dtype=jnp.int32)[None, None, :]
    key_pos = first - reach + column
    allowed = (
        (key_pos <= query_pos)
        & (key_pos > query_pos - reach)
        & (key_pos >= 0)
        & (query_pos - offset >= 0)
    )
    return allowed


def attend_block(query, key_one, value_one, key_two, value_two, valid):
    rows = query.shape[0]
    width = query.shape[1]
    spread = key_two.shape[1]
    mixed = (query[:, None, :].astype(jnp.float32) * key_two.astype(jnp.float32)).astype(
        jnp.bfloat16
    )
    scores = lax.dot_general(
        mixed.reshape(rows * spread, width),
        key_one,
        (((1,), (1,)), ((), ())),
        preferred_element_type=jnp.float32,
    )
    scores = scores.reshape(rows, spread, -1) * width ** (-0.5)
    scores = jnp.where(valid, scores, -jnp.inf)
    peak = jnp.max(scores, axis=(1, 2), keepdims=True)
    weights = jnp.exp(scores - peak)
    total = jnp.sum(weights, axis=(1, 2))
    blended = jnp.dot(
        weights.astype(jnp.bfloat16).reshape(rows * spread, -1),
        value_one,
        preferred_element_type=jnp.float32,
    )
    blended = blended.reshape(rows, spread, width)
    return jnp.sum(value_two.astype(jnp.float32) * blended, axis=1) / total[:, None]


def body(hidden_in, query_weight, shared_weight, out_weight, residual, norm_gain):
    tokens = hidden_in.shape[0]
    queries = jnp.dot(hidden_in, query_weight, preferred_element_type=jnp.float32).astype(
        jnp.bfloat16
    )
    shared = jnp.dot(
        hidden_in,
        lax.all_gather(shared_weight, "head", axis=1, tiled=True),
        preferred_element_type=jnp.float32,
    ).astype(jnp.bfloat16)
    first_pair = shared[:, : 2 * HD]
    second_pair = shared[:, 2 * HD :]
    reach = (W1 + tokens - 1) // tokens
    earlier, rim = from_behind((first_pair, second_pair[tokens - W2 :]), "ctx", 1)
    pieces = [earlier]
    for distance in range(2, reach + 1):
        pieces.append(from_behind(first_pair, "ctx", distance))
    extended_one = jnp.concatenate(pieces[::-1] + [first_pair], 0)
    extended_two = jnp.concatenate([rim, second_pair], 0)
    heads = queries.shape[1] // HD
    block = min(128, tokens)
    anchor = lax.axis_index("ctx") * tokens
    heads_q = queries.reshape(tokens, heads, HD).transpose(1, 0, 2)
    key_one = extended_one[:, :HD]
    value_one = extended_one[:, HD:]
    near = jnp.stack([extended_two[W2 - offset : W2 - offset + block] for offset in range(W2)], 1)
    key_two = near[:, :, :HD]
    value_two = near[:, :, HD:]
    valid = window_mask(anchor + 0, block, W2, W1)
    results = lax.map(
        lambda head: attend_block(head, key_one, value_one, key_two, value_two, valid), heads_q
    )
    attention = results.transpose(1, 0, 2).reshape(tokens, heads * HD).astype(jnp.bfloat16)
    summed = lax.psum_scatter(
        jnp.dot(attention, out_weight, preferred_element_type=jnp.float32),
        "head",
        scatter_dimension=0,
        tiled=True,
    )
    residual_out = (residual.astype(jnp.float32) + summed).astype(jnp.bfloat16)
    values = residual_out.astype(jnp.float32)
    scale = lax.rsqrt(jnp.mean(values * values, axis=1, keepdims=True) + 1e-05)
    normed_local = (values * scale * norm_gain).astype(jnp.bfloat16)
    normed = lax.all_gather(normed_local, "head", axis=0, tiled=True)
    return (residual_out, normed)


def solution(mesh):
    in_specs = (
        P("ctx", None),
        P(None, "head"),
        P(None, "head"),
        P("head", None),
        P(("ctx", "head"), None),
        P(),
    )
    out_specs = (P(("ctx", "head"), None), P("ctx", None))
    return jax.shard_map(body, mesh=mesh, in_specs=in_specs, out_specs=out_specs, check_vma=False)
```

profile of v0, /device:TPU:1, one launch (start us, length us, event | category | flops | bytes accessed | tf_op | source)
XLA Modules:
  0.0 247.0 jit_solution(3508131914323198901)
XLA Ops:
  7.2 0.0 all-gather.3.cloned.1.call-start
  7.2 0.7 all-gather.3.cloned.1.call-update
  7.9 0.0 reduce-scatter.2.cloned.1.call-start
  8.0 0.4 copy-done
  8.4 2.9 %fusion.17 = bf16[16,4,8,128]{3,2,1,0:T(8,128)(2,1)S(1)} fusion(bf16[128,4096]{1,0:T(8,128)(2,1)S(1)} %copy-done, bf16[4096,512]{1,0:T(8,128)(2,1)} %param.9), kind=kOutput, calls=%fused_computation.22 | convolution fusion | flops 536936448 | bytes 5373952 | tf_op jit(solution)/shard_map/dot_general | solution.py:60
  11.4 0.1 and_and_fusion
  11.6 42.5 %all-gather.3.cloned.1.call-done = bf16[4096,512]{0,1:T(8,128)(2,1)} async-done(((bf16[4096,32]{0,1:T(8,128)(2,1)}), bf16[4096,512]{0,1:T(8,128)(2,1)}) %all-gather.3.cloned.1.call-update) | async-done | bytes 4194320 | tf_op jit(solution)/shard_map/all_gather | solution.py:65
  54.0 3.7 %convolution_convert_fusion.1 = bf16[128,512]{1,0:T(8,128)(2,1)S(1)} fusion(bf16[128,4096]{1,0:T(8,128)(2,1)S(1)} %copy-done, bf16[4096,512]{0,1:T(8,128)(2,1)} %all-gather.3.cloned.1.call-done), kind=kOutput, calls=%fused_computation.21 | convolution fusion | flops 536936448 | bytes 5373952 | tf_op jit(solution)/shard_map/dot_general | solution.py:63
  57.7 7.4 %collective-permute-start.1 = (bf16[128,256]{1,0:T(8,128)(2,1)S(1)}, bf16[128,256]{1,0:T(8,128)(2,1)S(1)}, u32[]{:S(2)}, u32[]{:S(2)}) collective-permute-start(bf16[128,256]{1,0:T(8,128)(2,1)S(1)} %slice.217), channel_id=1, source_target_pairs={{0,64},{16,80},{32,96},{48,112},{64,128},{80,144},{96,160},{112,17... | collective-permute-start | bytes 196616 | tf_op jit(solution)/shard_map/ppermute | solution.py:14
  65.1 2.5 collective-permute-start.2
  67.6 4.7 %collective-permute-start.3 = (bf16[128,256]{1,0:T(8,128)(2,1)S(1)}, bf16[128,256]{1,0:T(8,128)(2,1)S(1)}, u32[]{:S(2)}, u32[]{:S(2)}) collective-permute-start(bf16[128,256]{1,0:T(8,128)(2,1)S(1)} %slice.217), channel_id=1, source_target_pairs={{0,32},{16,48},{32,64},{48,80},{64,96},{80,112},{96,128},{112,144}... | collective-permute-start | bytes 196616 | tf_op jit(solution)/shard_map/ppermute | solution.py:14
  72.3 3.2 %collective-permute-start.4 = (bf16[128,256]{1,0:T(8,128)(2,1)S(1)}, bf16[128,256]{1,0:T(8,128)(2,1)S(1)}, u32[]{:S(2)}, u32[]{:S(2)}) collective-permute-start(bf16[128,256]{1,0:T(8,128)(2,1)S(1)} %slice.217), channel_id=1, source_target_pairs={{0,16},{16,32},{32,48},{48,64},{64,80},{80,96},{96,112},{112,128},... | collective-permute-start | bytes 196616 | tf_op jit(solution)/shard_map/ppermute | solution.py:14
  75.5 3.2 %collective-permute-start = (bf16[32,256]{1,0:T(8,128)(2,1)S(1)}, bf16[32,256]{1,0:T(8,128)(2,1)S(1)}, u32[]{:S(2)}, u32[]{:S(2)}) collective-permute-start(bf16[32,256]{1,0:T(8,128)(2,1)S(1)} %slice.154), channel_id=1, source_target_pairs={{0,16},{16,32},{32,48},{48,64},{64,80},{80,96},{96,112},{112,128},... | collective-permute-start | bytes 49160 | tf_op jit(solution)/shard_map/ppermute | solution.py:14
  78.8 0.7 collective-permute-done
  80.4 0.6 fusion.82
  81.0 0.7 fusion.83
  81.7 49.9 %while.11 = (s32[]{:T(128)}, bf16[4,128,128]{1,2,0:T(8,128)(2,1)}, bf16[128,32,128]{2,0,1:T(8,128)(2,1)S(1)}, bf16[4,128,128]{2,1,0:T(8,128)(2,1)S(1)}, bf16[128...) while((s32[]{:T(128)}, bf16[4,128,128]{1,2,0:T(8,128)(2,1)}, ...), condition=%wide.region_4.5_spmd.clone, body=%wide.region_0.4_spmd.clone.sunk | while | flops 1382055680 | bytes 34602088 | solution.py:87
  81.7 3.4 %fusion.97 = (f32[128]{0:T(128)S(1)}, f32[128,32,640]{2,0,1:T(8,128)S(1)}) fusion(pred[128,32]{0,1:T(8,128)(4,1)S(1)} %get-tuple-element.183, pred[128,640]{1,0:T(8,128)(4,1)S(1)} %get-tuple-element.184, bf16[640,128]{1,0:T(8,128)(2,1)} %get-tuple-element.181, bf16[128,32,128]{2,0,1:T(8,128)(2,1)S(1)} %get-tuple-element.180, ...), kind=kOutput, calls=%fused_computation.5.clone.1 | convolution fusion | flops 683147136 | bytes 11850240 | tf_op jit(solution)/shard_map/while/body/eval_jaxpr/dot_general | solution.py:38
  85.1 3.5 %fusion.98 = f32[128]{0:T(128)S(1)} fusion(f32[128,32,640]{2,0,1:T(8,128)S(1)} %get-tuple-element.154, f32[128]{0:T(128)S(1)} %get-tuple-element.155, pred[128,32]{0,1:T(8,128)(4,1)S(1)} %get-tuple-element.183, pred[128,640]{1,0:T(8,128)(4,1)S(1)} %get-tuple-element.184), kind=kLoop, calls=%fused_computation.3.clone.1 | loop fusion | flops 13107072 | bytes 10572800 | tf_op jit(solution)/shard_map/while/body/eval_jaxpr/reduce_sum | solution.py:48
  88.7 4.7 %multiply_reduce_fusion.2 = f32[128,128]{1,0:T(8,128)S(1)} fusion(bf16[128,32,128]{2,0,1:T(8,128)(2,1)S(1)} %get-tuple-element.178, f32[128,32,640]{2,0,1:T(8,128)S(1)} %get-tuple-element.154, f32[128]{0:T(128)S(1)} %get-tuple-element.155, pred[128,32]{0,1:T(8,128)(4,1)S(1)} %get-tuple-element.183, pred[128,640]{1,0:T(8,128)(4,1)S(1)} %get-tuple-element.184, ...), kind=kOutput, calls=%fused_computation.9.clone.1 | convolution fusion | flops 685752320 | bytes 11850240 | tf_op jit(solution)/shard_map/while/body/eval_jaxpr/dot_general | solution.py:49
  93.3 0.1 bitcast_divide_fusion.2
  93.4 0.1 copy.18
  93.6 0.6 constant_dynamic-update-slice_fusion.39
  94.2 3.4 %fusion.97 = (f32[128]{0:T(128)S(1)}, f32[128,32,640]{2,0,1:T(8,128)S(1)}) fusion(pred[128,32]{0,1:T(8,128)(4,1)S(1)} %get-tuple-element.183, pred[128,640]{1,0:T(8,128)(4,1)S(1)} %get-tuple-element.184, bf16[640,128]{1,0:T(8,128)(2,1)} %get-tuple-element.181, bf16[128,32,128]{2,0,1:T(8,128)(2,1)S(1)} %get-tuple-element.180, ...), kind=kOutput, calls=%fused_computation.5.clone.1 | convolution fusion | flops 683147136 | bytes 11850240 | tf_op jit(solution)/shard_map/while/body/eval_jaxpr/dot_general | solution.py:38
  97.6 3.5 %fusion.98 = f32[128]{0:T(128)S(1)} fusion(f32[128,32,640]{2,0,1:T(8,128)S(1)} %get-tuple-element.154, f32[128]{0:T(128)S(1)} %get-tuple-element.155, pred[128,32]{0,1:T(8,128)(4,1)S(1)} %get-tuple-element.183, pred[128,640]{1,0:T(8,128)(4,1)S(1)} %get-tuple-element.184), kind=kLoop, calls=%fused_computation.3.clone.1 | loop fusion | flops 13107072 | bytes 10572800 | tf_op jit(solution)/shard_map/while/body/eval_jaxpr/reduce_sum | solution.py:48
  101.2 4.7 %multiply_reduce_fusion.2 = f32[128,128]{1,0:T(8,128)S(1)} fusion(bf16[128,32,128]{2,0,1:T(8,128)(2,1)S(1)} %get-tuple-element.178, f32[128,32,640]{2,0,1:T(8,128)S(1)} %get-tuple-element.154, f32[128]{0:T(128)S(1)} %get-tuple-element.155, pred[128,32]{0,1:T(8,128)(4,1)S(1)} %get-tuple-element.183, pred[128,640]{1,0:T(8,128)(4,1)S(1)} %get-tuple-element.184, ...), kind=kOutput, calls=%fused_computation.9.clone.1 | convolution fusion | flops 685752320 | bytes 11850240 | tf_op jit(solution)/shard_map/while/body/eval_jaxpr/dot_general | solution.py:49
  105.8 0.1 bitcast_divide_fusion.2
  105.9 0.1 copy.18
  106.0 0.6 constant_dynamic-update-slice_fusion.39
  106.7 3.4 %fusion.97 = (f32[128]{0:T(128)S(1)}, f32[128,32,640]{2,0,1:T(8,128)S(1)}) fusion(pred[128,32]{0,1:T(8,128)(4,1)S(1)} %get-tuple-element.183, pred[128,640]{1,0:T(8,128)(4,1)S(1)} %get-tuple-element.184, bf16[640,128]{1,0:T(8,128)(2,1)} %get-tuple-element.181, bf16[128,32,128]{2,0,1:T(8,128)(2,1)S(1)} %get-tuple-element.180, ...), kind=kOutput, calls=%fused_computation.5.clone.1 | convolution fusion | flops 683147136 | bytes 11850240 | tf_op jit(solution)/shard_map/while/body/eval_jaxpr/dot_general | solution.py:38
  110.1 3.5 %fusion.98 = f32[128]{0:T(128)S(1)} fusion(f32[128,32,640]{2,0,1:T(8,128)S(1)} %get-tuple-element.154, f32[128]{0:T(128)S(1)} %get-tuple-element.155, pred[128,32]{0,1:T(8,128)(4,1)S(1)} %get-tuple-element.183, pred[128,640]{1,0:T(8,128)(4,1)S(1)} %get-tuple-element.184), kind=kLoop, calls=%fused_computation.3.clone.1 | loop fusion | flops 13107072 | bytes 10572800 | tf_op jit(solution)/shard_map/while/body/eval_jaxpr/reduce_sum | solution.py:48
  113.6 4.7 %multiply_reduce_fusion.2 = f32[128,128]{1,0:T(8,128)S(1)} fusion(bf16[128,32,128]{2,0,1:T(8,128)(2,1)S(1)} %get-tuple-element.178, f32[128,32,640]{2,0,1:T(8,128)S(1)} %get-tuple-element.154, f32[128]{0:T(128)S(1)} %get-tuple-element.155, pred[128,32]{0,1:T(8,128)(4,1)S(1)} %get-tuple-element.183, pred[128,640]{1,0:T(8,128)(4,1)S(1)} %get-tuple-element.184, ...), kind=kOutput, calls=%fused_computation.9.clone.1 | convolution fusion | flops 685752320 | bytes 11850240 | tf_op jit(solution)/shard_map/while/body/eval_jaxpr/dot_general | solution.py:49
  118.3 0.1 bitcast_divide_fusion.2
  118.4 0.1 copy.18
  118.5 0.6 constant_dynamic-update-slice_fusion.39
  119.2 3.4 %fusion.97 = (f32[128]{0:T(128)S(1)}, f32[128,32,640]{2,0,1:T(8,128)S(1)}) fusion(pred[128,32]{0,1:T(8,128)(4,1)S(1)} %get-tuple-element.183, pred[128,640]{1,0:T(8,128)(4,1)S(1)} %get-tuple-element.184, bf16[640,128]{1,0:T(8,128)(2,1)} %get-tuple-element.181, bf16[128,32,128]{2,0,1:T(8,128)(2,1)S(1)} %get-tuple-element.180, ...), kind=kOutput, calls=%fused_computation.5.clone.1 | convolution fusion | flops 683147136 | bytes 11850240 | tf_op jit(solution)/shard_map/while/body/eval_jaxpr/dot_general | solution.py:38
  122.6 3.5 %fusion.98 = f32[128]{0:T(128)S(1)} fusion(f32[128,32,640]{2,0,1:T(8,128)S(1)} %get-tuple-element.154, f32[128]{0:T(128)S(1)} %get-tuple-element.155, pred[128,32]{0,1:T(8,128)(4,1)S(1)} %get-tuple-element.183, pred[128,640]{1,0:T(8,128)(4,1)S(1)} %get-tuple-element.184), kind=kLoop, calls=%fused_computation.3.clone.1 | loop fusion | flops 13107072 | bytes 10572800 | tf_op jit(solution)/shard_map/while/body/eval_jaxpr/reduce_sum | solution.py:48
  126.1 4.7 %multiply_reduce_fusion.2 = f32[128,128]{1,0:T(8,128)S(1)} fusion(bf16[128,32,128]{2,0,1:T(8,128)(2,1)S(1)} %get-tuple-element.178, f32[128,32,640]{2,0,1:T(8,128)S(1)} %get-tuple-element.154, f32[128]{0:T(128)S(1)} %get-tuple-element.155, pred[128,32]{0,1:T(8,128)(4,1)S(1)} %get-tuple-element.183, pred[128,640]{1,0:T(8,128)(4,1)S(1)} %get-tuple-element.184, ...), kind=kOutput, calls=%fused_computation.9.clone.1 | convolution fusion | flops 685752320 | bytes 11850240 | tf_op jit(solution)/shard_map/while/body/eval_jaxpr/dot_general | solution.py:49
  130.8 0.1 bitcast_divide_fusion.2
  130.9 0.1 copy.18
  131.0 0.6 constant_dynamic-update-slice_fusion.39
  131.6 4.3 %fusion.84 = f32[128,4096]{1,0:T(8,128)} fusion(bf16[128,512]{0,1:T(8,128)(2,1)} %bitcast.165, bf16[512,4096]{1,0:T(8,128)(2,1)} %param.11), kind=kOutput, calls=%fused_computation.168 | convolution fusion | flops 536870912 | bytes 6422528 | tf_op jit(solution)/shard_map/dot_general | solution.py:92
  136.0 0.0 all-gather.5.cloned.1.call-start
  136.0 62.4 %reduce-scatter.2.cloned.1.call-done = f32[8,4096]{1,0:T(8,128)} async-done(((f32[128,4096]{1,0:T(8,128)}), f32[8,4096]{1,0:T(8,128)}) %reduce-scatter.2.cloned.1.call-update) | async-done | bytes 131088 | tf_op jit(solution)/shard_map/reduce_scatter | solution.py:91
  198.4 1.1 fusion.18
  199.5 0.7 fusion.20
  200.2 37.9 %all-gather.5.cloned.1.call-done = bf16[128,4096]{1,0:T(8,128)(2,1)} async-done(((bf16[8,4096]{1,0:T(8,128)(2,1)}), bf16[128,4096]{1,0:T(8,128)(2,1)}) %all-gather.5.cloned.1.call-update) | async-done | bytes 1048592 | tf_op jit(solution)/shard_map/all_gather | solution.py:101
  238.2 2.3 copy.64
  (63 shorter events, 0.8 us)
Async XLA Ops:
  7.2 1.2 copy-start
  7.2 46.8 %all-gather.3.cloned.1.call-start = ((), (), s32[]{:S(2)}) async-start(), calls=%async_computation.1 | async-start | bytes 4456448 | tf_op jit(solution)/shard_map/all_gather | solution.py:65
  7.9 190.5 %reduce-scatter.2.cloned.1.call-start = ((), (), s32[]{:S(2)}) async-start(), calls=%async_computation.2 | async-start | bytes 2228224 | tf_op jit(solution)/shard_map/reduce_scatter | solution.py:91
  57.7 20.9 %collective-permute-start.1 = (bf16[128,256]{1,0:T(8,128)(2,1)S(1)}, bf16[128,256]{1,0:T(8,128)(2,1)S(1)}, u32[]{:S(2)}, u32[]{:S(2)}) collective-permute-start(bf16[128,256]{1,0:T(8,128)(2,1)S(1)} %slice.217), channel_id=1, source_target_pairs={{0,64},{16,80},{32,96},{48,112},{64,128},{80,144},{96,160},{112,17... | collective-permute-start | bytes 196616 | tf_op jit(solution)/shard_map/ppermute | solution.py:14
  65.1 13.6 %collective-permute-start.2 = (bf16[128,256]{1,0:T(8,128)(2,1)S(1)}, bf16[128,256]{1,0:T(8,128)(2,1)S(1)}, u32[]{:S(2)}, u32[]{:S(2)}) collective-permute-start(bf16[128,256]{1,0:T(8,128)(2,1)S(1)} %slice.217), channel_id=1, source_target_pairs={{0,48},{16,64},{32,80},{48,96},{64,112},{80,128},{96,144},{112,160... | collective-permute-start | bytes 196616 | tf_op jit(solution)/shard_map/ppermute | solution.py:14
  67.6 11.1 %collective-permute-start.3 = (bf16[128,256]{1,0:T(8,128)(2,1)S(1)}, bf16[128,256]{1,0:T(8,128)(2,1)S(1)}, u32[]{:S(2)}, u32[]{:S(2)}) collective-permute-start(bf16[128,256]{1,0:T(8,128)(2,1)S(1)} %slice.217), channel_id=1, source_target_pairs={{0,32},{16,48},{32,64},{48,80},{64,96},{80,112},{96,128},{112,144}... | collective-permute-start | bytes 196616 | tf_op jit(solution)/shard_map/ppermute | solution.py:14
  72.3 6.5 %collective-permute-start.4 = (bf16[128,256]{1,0:T(8,128)(2,1)S(1)}, bf16[128,256]{1,0:T(8,128)(2,1)S(1)}, u32[]{:S(2)}, u32[]{:S(2)}) collective-permute-start(bf16[128,256]{1,0:T(8,128)(2,1)S(1)} %slice.217), channel_id=1, source_target_pairs={{0,16},{16,32},{32,48},{48,64},{64,80},{80,96},{96,112},{112,128},... | collective-permute-start | bytes 196616 | tf_op jit(solution)/shard_map/ppermute | solution.py:14
  75.5 4.0 %collective-permute-start = (bf16[32,256]{1,0:T(8,128)(2,1)S(1)}, bf16[32,256]{1,0:T(8,128)(2,1)S(1)}, u32[]{:S(2)}, u32[]{:S(2)}) collective-permute-start(bf16[32,256]{1,0:T(8,128)(2,1)S(1)} %slice.154), channel_id=1, source_target_pairs={{0,16},{16,32},{32,48},{48,64},{64,80},{80,96},{96,112},{112,128},... | collective-permute-start | bytes 49160 | tf_op jit(solution)/shard_map/ppermute | solution.py:14
  136.0 62.4 %copy-start.2 = (bf16[8,4096]{1,0:T(8,128)(2,1)S(1)}, bf16[8,4096]{1,0:T(8,128)(2,1)}, u32[]{:S(2)}) copy-start(bf16[8,4096]{1,0:T(8,128)(2,1)} %param.12) | copy-start | bytes 196612
  136.0 63.5 %copy-start.3 = (f32[4096]{0:T(1024)S(1)}, f32[4096]{0:T(1024)}, u32[]{:S(2)}) copy-start(f32[4096]{0:T(1024)} %param.13) | copy-start | bytes 49156
  136.0 102.2 %all-gather.5.cloned.1.call-start = ((), (), s32[]{:S(2)}) async-start(), calls=%async_computation.3 | async-start | bytes 1114112 | tf_op jit(solution)/shard_map/all_gather | solution.py:101
  199.5 41.0 %copy-start.1 = (bf16[8,4096]{1,0:T(8,128)(2,1)}, bf16[8,4096]{1,0:T(8,128)(2,1)S(1)}, u32[]{:S(2)}) copy-start(bf16[8,4096]{1,0:T(8,128)(2,1)S(1)} %get-tuple-element.188) | copy-start | bytes 196612
Sparse Core Ops, SparseCore 0:
  9.9 44.0 all-gather.2
  136.1 62.2 reduce-scatter.1
  200.8 37.2 all-gather.4
where the time goes:
time: 248 us; the launch traced here: 247 us
  waiting for transfers between devices  144 us (58%)
  matrix products  43.3 us (17%)
  starting transfers between devices  21 us (8%)
  other arithmetic  17 us (7%)
  between operations  14.2 us (6%)
  local copies, waits for them, and re-layouts  7.07 us (3%)
    reduce_scatter x1, waiting for transfers between devices, body(): lax.psum_scatter(jnp.dot(attention, out_weight, preferred_element_type=jn...  62.4 us
    all_gather x1, waiting for transfers between devices, body(): lax.all_gather(shared_weight, 'head', axis=1, tiled=True)  42.5 us
    all_gather x1, waiting for transfers between devices, body(): normed = lax.all_gather(normed_local, 'head', axis=0, tiled=True)  37.9 us
    ppermute x5, starting transfers between devices, from_behind(): lax.ppermute(value, axis, [(source, source + steps) for source in range(i...  20.9 us
    dot_general x4, matrix products, attend_block(): jnp.dot(weights.astype(jnp.bfloat16).reshape(rows * spread, -1), value_on...  18.7 us
    reduce_sum x4, other arithmetic, attend_block(): total = jnp.sum(weights, axis=(1, 2))  14.1 us
    dot_general x4, matrix products, attend_block(): lax.dot_general(mixed.reshape(rows * spread, width), key_one, (((1,), (1,...  13.7 us
  transfers between devices with their start and end apart: 8, of which 4 were waited for; matrix products, arithmetic and copies ran while one was open for 1% of the time, Pallas kernels for 0%

commit v1 on v0

v1 whole, which is shorter than its diff:
```python
import functools
import math

import jax
import jax.numpy as jnp
from jax import lax
from jax.experimental import pallas as pl
from jax.experimental.pallas import tpu as pltpu
from jax.sharding import PartitionSpec as P

HD = 128
W1 = 512
W2 = 32
TB = 16
T = 32
REACH = 4
MESH = pl.DeviceIdType.MESH
SCALE = HD**-0.5 * math.log2(math.e)


def kernel(
    hidden_hbm, qw_hbm, sw_hbm, ow_hbm, residual_hbm, gain_hbm,
    rout_ref, normed_hbm,
    hidden, qw, sw, ow, residual, gain,
    kv1, kv2, keys, values, k2e, k2s, v2s, qs, att, sa, sb,
    psib, pown, r1, r2s, r2, ro, nrm,
    load_sem, qw_sem, out_sem,
    a_send, a1_recv, a2_recv, b_send, b1_recv, b2_recv, c_send, c1_recv, c2_recv,
    r1_send, r1_recv, r2_send, r2_recv, ag_send, ag_recv, sh_send, sh_recv,
):
    n_ctx = lax.axis_size("ctx")
    ctx = lax.axis_index("ctx")
    head = lax.axis_index("head")
    core = lax.rem(head, 2)
    chip = head // 2
    y = lax.rem(chip, 4)
    x_lo = chip // 4
    slot = pl.multiple_of(lax.rem(head, 8) * 32, 32)
    tokens, width = hidden_hbm.shape
    heads = qw_hbm.shape[1] // HD
    n_blocks = tokens // T
    steps = tokens // TB
    chunk = width // 16
    sibling = chip * 2 + 1 - core

    def load(src, dst, sem):
        return pltpu.make_async_copy(src, dst, sem)

    parts = 4
    deep = width // parts
    loads = [
        load(hidden_hbm, hidden, load_sem.at[0]),
        load(sw_hbm, sw, load_sem.at[1]),
        load(residual_hbm, residual, load_sem.at[2]),
        load(gain_hbm, gain, load_sem.at[3]),
        load(ow_hbm, ow, load_sem.at[4]),
    ]
    qw_loads = [
        load(qw_hbm.at[pl.ds(k * deep, deep)], qw.at[pl.ds(k * deep, deep)], qw_sem.at[k])
        for k in range(parts)
    ]
    loads[0].start()
    loads[1].start()
    for item in qw_loads:
        item.start()
    for item in loads[2:]:
        item.start()

    def push(src, dst, send, recv, to):
        return pltpu.make_async_remote_copy(
            src_ref=src, dst_ref=dst, send_sem=send, recv_sem=recv, device_id=to, device_id_type=MESH
        )

    barrier = pltpu.get_barrier_semaphore()
    for d in range(1, REACH + 1):
        for xt in range(2):
            pl.semaphore_signal(
                barrier, inc=1, device_id=(lax.rem(ctx + n_ctx - d, n_ctx), xt * 8 + lax.rem(head, 8)),
                device_id_type=MESH,
            )
    for k in range(1, 8):
        pl.semaphore_signal(
            barrier, inc=1, device_id=(ctx, lax.rem(chip + k, 8) * 2 + core), device_id_type=MESH
        )
    pl.semaphore_signal(barrier, inc=1, device_id=(ctx, sibling), device_id_type=MESH)

    loads[0].wait()
    loads[1].wait()
    part = jnp.dot(hidden[...], sw[...], preferred_element_type=jnp.float32)
    part = part.astype(jnp.bfloat16).astype(jnp.float32)
    part = jnp.concatenate([part, jnp.zeros((tokens, HD - 32), jnp.float32)], axis=1)
    part = part.T[:32].astype(jnp.bfloat16)

    mine = pl.ds(slot, 32)

    @pl.when(x_lo == 0)
    def _():
        kv1[0, mine, :] = part

    @pl.when(x_lo == 1)
    def _():
        kv2[0, mine, :] = part

    pl.semaphore_wait(barrier, 2 * REACH + 8)

    def a_copy(buf, recv, d, xt):
        return push(
            buf.at[0, mine], buf.at[d, mine], a_send.at[d, xt], recv.at[d],
            (lax.rem(ctx + d, n_ctx), xt * 8 + lax.rem(head, 8)),
        )

    first_sends = [(0, 1)] + [(d, xt) for d in range(1, REACH + 1) for xt in range(2)]
    second_sends = [(0, 0)] + [(1, xt) for xt in range(2)]

    @pl.when(x_lo == 0)
    def _():
        for d, xt in first_sends:
            a_copy(kv1, a1_recv, d, xt).start()

    @pl.when(x_lo == 1)
    def _():
        for d, xt in second_sends:
            a_copy(kv2, a2_recv, d, xt).start()

    def project(ks):
        total = None
        for k in ks:
            qw_loads[k].wait()
            term = jnp.dot(
                hidden[:, k * deep : (k + 1) * deep], qw[k * deep : (k + 1) * deep, :],
                preferred_element_type=jnp.float32,
            )
            total = term if total is None else total + term
        return total

    half = project((0, 1))
    sa[0:tokens, 0 : heads * HD] = half

    for d in range(1, REACH + 1):
        a_copy(kv1, a1_recv, d, 0).wait_recv()
    a_copy(kv2, a2_recv, 1, 0).wait_recv()

    @pl.when(x_lo == 1)
    def _():
        a_copy(kv1, a1_recv, 0, 0).wait_recv()

    @pl.when(x_lo == 0)
    def _():
        a_copy(kv2, a2_recv, 0, 0).wait_recv()

    def b_copy(which, k):
        buf, recv = ((kv1, b1_recv), (kv2, b2_recv))[which]
        return push(
            buf.at[:, mine], buf.at[:, mine], b_send.at[which, k], recv.at[k],
            (ctx, x_lo * 8 + lax.rem(y + k, 4) * 2 + core),
        )

    def c_copy(which, k):
        buf, recv = ((kv1, c1_recv), (kv2, c2_recv))[which]
        rows = pl.ds(pl.multiple_of((lax.rem(y + 4 - k, 4) * 2 + core) * 32, 32), 32)
        return push(buf.at[:, rows], buf.at[:, rows], c_send.at[which, k], recv.at[k], (ctx, sibling))

    for k in (1, 3, 2):
        for which in (1, 0):
            b_copy(which, k).start()
    for which in (1, 0):
        c_copy(which, 0).start()

    qs[...] = (sa[0:tokens, 0 : heads * HD] + project((2, 3))).astype(jnp.bfloat16)

    for k in (1, 3, 2):
        for which in (1, 0):
            b_copy(which, k).wait_recv()
            c_copy(which, k).start()
    for k in (0, 1, 3, 2):
        c_copy(1, k).wait_recv()

    t_iota = lax.broadcasted_iota(jnp.int32, (tokens, HD), 0)
    for which, dst in ((0, k2s), (1, v2s)):
        rows = slice(which * HD, (which + 1) * HD)
        k2e[0:W2] = kv2[1, rows, :].astype(jnp.float32).T[tokens - W2 :]
        k2e[W2 : W2 + tokens] = kv2[0, rows, :].astype(jnp.float32).T
        for r in range(W2):
            moved = k2e[W2 - r : W2 - r + tokens]
            if r:
                other = k2e[W2 : W2 + tokens] if which == 0 else jnp.zeros_like(moved)
                moved = jnp.where((ctx > 0) | (t_iota >= r), moved, other)
            dst[r] = moved.astype(jnp.bfloat16)

    for k in (0, 1, 3, 2):
        c_copy(0, k).wait_recv()

    own_key = kv1[0, 0:HD, :].astype(jnp.float32) * SCALE
    for d in range(REACH + 1):
        cols = slice((REACH - d) * HD, (REACH - d + 1) * HD)
        key = kv1[d, 0:HD, :].astype(jnp.float32) * SCALE
        value = kv1[d, HD : 2 * HD, :].astype(jnp.float32).T
        ones = jnp.ones((HD, HD), jnp.float32)
        if d:
            here = ctx >= d
            key = jnp.where(here, key, own_key[:, 0:1])
            value = jnp.where(here, value, 0.0)
            ones = jnp.where(here, ones, 0.0)
        high = key.astype(jnp.bfloat16)
        keys[0:HD, cols] = high
        keys[HD : 2 * HD, cols] = (key - high.astype(jnp.float32)).astype(jnp.bfloat16)
        values[cols, 0:HD] = value.astype(jnp.bfloat16)
        values[cols, HD : 2 * HD] = ones.astype(jnp.bfloat16)

    for item in loads[2:]:
        item.wait()

    def scores(h, t0):
        q = qs[pl.ds(t0, TB), h * HD : (h + 1) * HD]
        mixed = (k2s[:, pl.ds(t0, TB), :] * q[None]).reshape(W2 * TB, HD)
        mixed = jnp.concatenate([mixed, mixed], axis=1)
        return jnp.dot(mixed, keys[...], preferred_element_type=jnp.float32)

    def attend(buf, h, t0):
        n = W2 * TB
        s = buf[...].reshape(W2, TB, 5 * HD)
        tok = t0 + lax.broadcasted_iota(jnp.int32, (TB, HD), 0)
        col = lax.broadcasted_iota(jnp.int32, (TB, HD), 1)
        new = (col <= tok)[None]
        both = jnp.where(new, s[:, :, 512:], s[:, :, :128])
        peak = jnp.maximum(
            jnp.maximum(both, s[:, :, 128:256]), jnp.maximum(s[:, :, 256:384], s[:, :, 384:512])
        )
        peak = jnp.max(jnp.max(peak, axis=0), axis=1, keepdims=True)[None]
        shared_w = jnp.exp2(both - peak).astype(jnp.bfloat16).reshape(n, HD)
        newb = jnp.broadcast_to(new, (W2, TB, HD)).reshape(n, HD)
        w_old = jnp.where(newb, 0, shared_w)
        w_new = jnp.where(newb, shared_w, 0)
        w_mid = jnp.exp2(s[:, :, 128:512] - peak).astype(jnp.bfloat16).reshape(n, 3 * HD)
        w = jnp.concatenate([w_old, w_mid, w_new], axis=1)
        o = jnp.dot(w, values[...], preferred_element_type=jnp.float32).reshape(W2, TB, 2 * HD)
        num = jnp.sum(o[:, :, :HD] * v2s[:, pl.ds(t0, TB), :].astype(jnp.float32), axis=0)
        missing = jnp.where(ctx > 0, 0, jnp.maximum(W2 - 1 - tok, 0)).astype(jnp.float32)
        den = jnp.sum(o[:, :, HD:], axis=0) - missing * o[0, :, HD:]
        att[pl.ds(t0, TB), h * HD : (h + 1) * HD] = (num / den).astype(jnp.bfloat16)

    bufs = (sa, sb)
    sa[...] = scores(0, 0)

    def r1_copy(b):
        return push(psib.at[b], r1.at[b], r1_send.at[b], r1_recv.at[b], (ctx, sibling))

    def r2_copy(b, k):
        to = lax.rem(chip + k, 8)
        return push(
            r2s.at[b, to], r2.at[b, k - 1], r2_send.at[b, k - 1], r2_recv.at[b, k - 1], (ctx, to * 2 + core)
        )

    def rows_of(b):
        return pl.ds(pl.multiple_of(b * T, T), T)

    def ag_copy(b, k):
        to = lax.rem(chip + k, 8)
        piece = ro.at[core, chip, rows_of(b)]
        return push(piece, piece, ag_send.at[b, k - 1], ag_recv.at[b, k - 1], (ctx, to * 2 + core))

    def sh_copy(b):
        piece = ro.at[core, :, rows_of(b)]
        return push(piece, piece, sh_send.at[b], sh_recv.at[b], (ctx, sibling))

    def out_copy(b):
        return pltpu.make_async_copy(nrm.at[rows_of(b)], normed_hbm.at[rows_of(b)], out_sem.at[b])

    def product(b, to, to_core):
        cols = pl.ds(pl.multiple_of((to * 2 + to_core) * chunk, chunk), chunk)
        p = jnp.dot(att[rows_of(b), :], ow[:, cols], preferred_element_type=jnp.float32)
        row = lax.broadcasted_iota(jnp.int32, (T, chunk), 0) + (b * T - 8 * head)
        res = residual[:, cols].astype(jnp.float32)
        return p + jnp.where((row >= 0) & (row < 8), jnp.concatenate([res] * (T // 8), axis=0), 0.0)

    def event_project(b):
        def for_sibling(to, _):
            psib[b, to] = product(b, to, 1 - core).astype(jnp.bfloat16)
            return 0

        lax.fori_loop(0, 8, for_sibling, 0)
        r1_copy(b).start()

        def for_self(to, _):
            pown[b, to] = product(b, to, core)
            return 0

        lax.fori_loop(0, 8, for_self, 0)

    def event_scatter(b):
        r1_copy(b).wait_recv()
        for k in (6, 2, 5, 3, 7, 1, 4):
            to = lax.rem(chip + k, 8)
            r2s[b, to] = (pown[b, to] + r1[b, to].astype(jnp.float32)).astype(jnp.bfloat16)
            r2_copy(b, k).start()

    def event_reduce(b):
        total = pown[b, chip] + r1[b, chip].astype(jnp.float32)
        for k in range(1, 8):
            r2_copy(b, k).wait_recv()
        for k in range(1, 8):
            total = total + r2[b, k - 1].astype(jnp.float32)
        ro[core, chip, rows_of(b), :] = total.astype(jnp.bfloat16)
        for k in (6, 2, 5, 3, 7, 1, 4):
            ag_copy(b, k).start()

    def event_share(b):
        for k in range(1, 8):
            to = lax.rem(chip + 8 - k, 8)
            piece = ro.at[core, to, rows_of(b)]
            push(piece, piece, ag_send.at[b, k - 1], ag_recv.at[b, k - 1], (ctx, to * 2 + core)).wait_recv()
        sh_copy(b).start()

    def event_norm(b):
        piece = ro.at[1 - core, :, rows_of(b)]
        push(piece, piece, sh_send.at[b], sh_recv.at[b], (ctx, sibling)).wait_recv()
        square = jnp.zeros((T, chunk), jnp.float32)
        for c in range(2):
            for to in range(8):
                v = ro[c, to, rows_of(b), :].astype(jnp.float32)
                square = square + v * v
        scale = lax.rsqrt(jnp.sum(square, axis=1, keepdims=True) * (1.0 / width) + 1e-05)
        for c in range(2):
            for to in range(8):
                cols = slice((to * 2 + c) * chunk, (to * 2 + c + 1) * chunk)
                v = ro[c, to, rows_of(b), :].astype(jnp.float32)
                nrm[rows_of(b), cols] = (v * scale * gain[:, cols]).astype(jnp.bfloat16)
        out_copy(b).start()

    per = T // TB

    def step(i, _):
        @pl.when(i < steps)
        def _():
            t0 = pl.multiple_of(i * TB, TB)
            later = pl.multiple_of(jnp.minimum(i + 1, steps - 1) * TB, TB)
            for h in range(heads):
                nxt = bufs[(h + 1) % 2]
                if h + 1 < heads:
                    nxt[...] = scores(h + 1, t0)
                else:
                    nxt[...] = scores(0, later)
                attend(bufs[h % 2], h, t0)

        def at(lag, event):
            j = i + 1 - lag
            b = j // per

            @pl.when((j >= per) & (lax.rem(j, per) == 0) & (b <= n_blocks))
            def _():
                event(b - 1)

        at(4, event_norm)
        at(3, event_share)
        at(2, event_reduce)
        at(1, event_scatter)
        at(0, event_project)
        return 0

    lax.fori_loop(0, steps + 4, step, 0)

    for c in range(2):
        for to in range(8):
            cols = slice((to * 2 + c) * chunk, (to * 2 + c + 1) * chunk)
            v = ro[c, to, pl.ds(pl.multiple_of(head // 2 * 16, 16), 16), :].astype(jnp.float32)
            rout_ref[:, cols] = jnp.where(lax.rem(head, 2) == 0, v[:8], v[8:]).astype(jnp.bfloat16)

    @pl.when(x_lo == 0)
    def _():
        for d, xt in first_sends:
            a_copy(kv1, a1_recv, d, xt).wait_send()

    @pl.when(x_lo == 1)
    def _():
        for d, xt in second_sends:
            a_copy(kv2, a2_recv, d, xt).wait_send()

    for which in range(2):
        for k in range(1, 4):
            b_copy(which, k).wait_send()
        for k in range(4):
            c_copy(which, k).wait_send()

    def finish(b, _):
        r1_copy(b).wait_send()
        for k in range(1, 8):
            r2_copy(b, k).wait_send()
            ag_copy(b, k).wait_send()
        sh_copy(b).wait_send()
        out_copy(b).wait()
        return 0

    lax.fori_loop(0, n_blocks, finish, 0)


def body(hidden_in, query_weight, shared_weight, out_weight, residual, norm_gain):
    tokens, width = hidden_in.shape
    columns = query_weight.shape[1]
    blocks = tokens // T
    chunk = width // 16
    vmem = lambda shape, dtype=jnp.bfloat16: pltpu.VMEM(shape, dtype)
    dma = lambda *shape: pltpu.SemaphoreType.DMA(shape)
    anywhere = pl.BlockSpec(memory_space=pl.ANY)
    rows = W2 * TB
    rout, normed = pl.pallas_call(
        kernel,
        out_shape=(
            jax.ShapeDtypeStruct(residual.shape, jnp.bfloat16),
            jax.ShapeDtypeStruct(hidden_in.shape, jnp.bfloat16),
        ),
        in_specs=[anywhere] * 6,
        out_specs=(pl.BlockSpec(memory_space=pltpu.VMEM), anywhere),
        scratch_shapes=[
            vmem((tokens, width)),
            vmem((width, columns)),
            vmem(shared_weight.shape),
            vmem(out_weight.shape),
            vmem(residual.shape),
            vmem((1, width), jnp.float32),
            vmem((REACH + 1, 2 * HD, tokens)),
            vmem((2, 2 * HD, tokens)),
            vmem((2 * HD, (REACH + 1) * HD)),
            vmem(((REACH + 1) * HD, 2 * HD)),
            vmem((W2 + tokens, HD), jnp.float32),
            vmem((W2, tokens, HD)),
            vmem((W2, tokens, HD)),
            vmem((tokens, columns)),
            vmem((tokens, columns)),
            vmem((rows, (REACH + 1) * HD), jnp.float32),
            vmem((rows, (REACH + 1) * HD), jnp.float32),
            vmem((blocks, 8, T, chunk)),
            vmem((blocks, 8, T, chunk), jnp.float32),
            vmem((blocks, 8, T, chunk)),
            vmem((blocks, 8, T, chunk)),
            vmem((blocks, 7, T, chunk)),
            vmem((2, 8, tokens, chunk)),
            vmem((tokens, width)),
            dma(5), dma(4), dma(blocks),
            dma(REACH + 1, 2), dma(REACH + 1), dma(2),
            dma(2, 4), dma(4), dma(4),
            dma(2, 4), dma(4), dma(4),
            dma(blocks), dma(blocks),
            dma(blocks, 7), dma(blocks, 7),
            dma(blocks, 7), dma(blocks, 7),
            dma(blocks), dma(blocks),
        ],
        compiler_params=pltpu.CompilerParams(
            collective_id=0, has_side_effects=True, vmem_limit_bytes=56 * 2**20
        ),
    )(hidden_in, query_weight, shared_weight, out_weight, residual, norm_gain.reshape(1, width))
    return rout, normed


def solution(mesh):
    in_specs = (
        P("ctx", None),
        P(None, "head"),
        P(None, "head"),
        P("head", None),
        P(("ctx", "head"), None),
        P(),
    )
    out_specs = (P(("ctx", "head"), None), P("ctx", None))
    return jax.shard_map(body, mesh=mesh, in_specs=in_specs, out_specs=out_specs, check_vma=False)
```

time: 248 us -> 77.6 us (0.31)
  waiting for transfers between devices: 144 us -> 0 us
  Pallas kernels: 0 us -> 70.7 us
  matrix products: 43.3 us -> 0 us
  starting transfers between devices: 21 us -> 0 us
  other arithmetic: 17 us -> 0 us
  between operations: 14.2 us -> 0.64 us
    all_gather x2 -> x0, waiting for transfers between devices: 80.4 us -> none  [the longest x1 42.5 us: body(): lax.all_gather(shared_weight, 'head', axis=1, tiled=True)]
    pallas_call x0 -> x1, Pallas kernels: none -> 70.7 us  [body(): pl.pallas_call(kernel, out_shape=(jax.ShapeDtypeStruct(residual.shape, jn...]
    reduce_scatter x1 -> x0, waiting for transfers between devices: 62.4 us -> none  [body(): lax.psum_scatter(jnp.dot(attention, out_weight, preferred_element_type=jn...]
    dot_general x11 -> x0, matrix products: 43.3 us -> none  [the longest x4 18.7 us: attend_block(): jnp.dot(weights.astype(jnp.bfloat16).reshape(rows * spread, -1), value_on...]
    ppermute x5 -> x0, starting transfers between devices: 20.9 us -> none  [from_behind(): lax.ppermute(value, axis, [(source, source + steps) for source in range(i...]
    reduce_sum x5 -> x0, other arithmetic: 15.1 us -> none  [the longest x4 14.1 us: attend_block(): total = jnp.sum(weights, axis=(1, 2))]
    unnamed x14 -> x3, local copies, waits for them, and re-layouts: 2.75 us -> 6.03 us
    dynamic_update_slice x8 -> x0, local copies, waits for them, and re-layouts: 2.94 us -> none  [body(): lax.map(lambda head: attend_block(head, key_one, value_one, key_two, valu...]
  transfers between devices with their start and end apart: 8 -> 0, of which waited for: 4 -> 0; matrix products, arithmetic and copies ran while one was open for 1% -> 0% of each run, Pallas kernels for 0% -> 0%
where the time goes in v1:
time: 77.6 us; the launch traced here: 77.4 us
  Pallas kernels  70.7 us (91%)
  local copies, waits for them, and re-layouts  6.03 us (8%)
    pallas_call x1, Pallas kernels, body(): pl.pallas_call(kernel, out_shape=(jax.ShapeDtypeStruct(residual.shape, jn...  70.7 us
    unnamed x3, local copies, waits for them, and re-layouts  6.03 us

profile of v1, /device:TPU:1, one launch (start us, length us, event | category | flops | bytes accessed | tf_op | source)
XLA Modules:
  0.0 77.4 jit_solution(8899830165178805000)
XLA Ops:
  0.6 2.3 %copy.8.sw_hbm = bf16[4096,32]{1,0:T(8,128)(2,1)} copy(bf16[4096,32]{0,1:T(8,128)(2,1)} %param.8) | data formatting | bytes 524288 | tf_op args[2]
  2.9 70.7 %shard_map.77 = (bf16[8,4096]{1,0:T(8,128)(2,1)}, bf16[128,4096]{1,0:T(8,128)(2,1)}) custom-call(bf16[128,4096]{1,0:T(8,128)(2,1)} %hidden_hbm.1, bf16[4096,512]{1,0:T(8,128)(2,1)} %qw_hbm.1, bf16[4096,32]{1,0:T(8,128)(2,1)} %copy.8.sw_hbm, bf16[512,4096]{1,0:T(8,128)(2,1)} %ow_hbm.1, bf16[8,4096]{1,0:T(8,128)(2,1)} %residual_hbm.1, f32[1,4096]{1,0:T(1,128)} %bitcast.1), custom_call_target="tpu_custom_call" | custom-call | tf_op jit(solution)/shard_map/pallas_call | solution.py:405
  73.6 1.5 %copy.11 = bf16[8,4096]{1,0:T(8,128)(2,1)} copy(bf16[8,4096]{1,0:T(8,128)(2,1)} %get-tuple-element.4) | data formatting | bytes 131072
  75.1 2.3 %copy.12 = bf16[128,4096]{1,0:T(8,128)(2,1)} copy(bf16[128,4096]{1,0:T(8,128)(2,1)} %get-tuple-element.5) | data formatting | bytes 2097152

commit v2 on v1

v2 whole, which is shorter than its diff:
```python
import functools
import math

import jax
import jax.numpy as jnp
from jax import lax
from jax.experimental import pallas as pl
from jax.experimental.pallas import tpu as pltpu
from jax.sharding import PartitionSpec as P

HD = 128
W1 = 512
W2 = 32
TB = 16
T = 32
REACH = 4
LAGS = (1, 4, 7, 8)
MESH = pl.DeviceIdType.MESH
SCALE = HD**-0.5 * math.log2(math.e)


def kernel(
    hidden_hbm, qw_hbm, sw_hbm, ow_hbm, residual_hbm,
    ro_hbm,
    hidden, qw, sw, ow, residual,
    kv, keys, keys_new, values, values_last, k2e, k2s, v2s, qs, att, sa, na, sb, nb,
    psib, pown, r1, r2s, r2, ro,
    load_sem, qw_sem, out_sem,
    a_send, a_recv, b_send, b_recv, c_send, c_recv,
    r1_send, r1_recv, r2_send, r2_recv, ag_send, ag_recv, sh_send, sh_recv,
):
    n_ctx = lax.axis_size("ctx")
    ctx = lax.axis_index("ctx")
    head = lax.axis_index("head")
    core = lax.rem(head, 2)
    chip = head // 2
    y = lax.rem(chip, 4)
    x_lo = chip // 4
    tokens, width = hidden_hbm.shape
    heads = qw_hbm.shape[1] // HD
    n_blocks = tokens // T
    steps = tokens // TB
    chunk = width // 16
    sibling = chip * 2 + 1 - core

    def load(src, dst, sem):
        return pltpu.make_async_copy(src, dst, sem)

    parts = 4
    deep = width // parts
    loads = [
        load(hidden_hbm, hidden, load_sem.at[0]),
        load(sw_hbm, sw, load_sem.at[1]),
        load(residual_hbm, residual, load_sem.at[2]),
        load(ow_hbm, ow, load_sem.at[3]),
    ]
    qw_loads = [
        load(qw_hbm.at[pl.ds(k * deep, deep)], qw.at[pl.ds(k * deep, deep)], qw_sem.at[k])
        for k in range(parts)
    ]
    loads[0].start()
    loads[1].start()

    def push(src, dst, send, recv, to):
        return pltpu.make_async_remote_copy(
            src_ref=src, dst_ref=dst, send_sem=send, recv_sem=recv, device_id=to, device_id_type=MESH
        )

    barrier = pltpu.get_barrier_semaphore()
    for d in range(1, REACH + 1):
        for xt in range(2):
            pl.semaphore_signal(
                barrier, inc=1, device_id=(lax.rem(ctx + n_ctx - d, n_ctx), xt * 8 + lax.rem(head, 8)),
                device_id_type=MESH,
            )
    for k in range(1, 8):
        pl.semaphore_signal(
            barrier, inc=1, device_id=(ctx, lax.rem(chip + k, 8) * 2 + core), device_id_type=MESH
        )
    pl.semaphore_signal(barrier, inc=1, device_id=(ctx, sibling), device_id_type=MESH)

    loads[0].wait()
    loads[1].wait()
    for item in qw_loads:
        item.start()
    for item in loads[2:]:
        item.start()
    part = lax.dot_general(
        hidden[...], sw[...], (((1,), (1,)), ((), ())), preferred_element_type=jnp.float32
    )
    part = part.astype(jnp.bfloat16).astype(jnp.float32)
    part = jnp.concatenate([part, jnp.zeros((tokens, HD - 32), jnp.float32)], axis=1)
    part = part.T[:32].astype(jnp.bfloat16)

    @pl.when(x_lo == 0)
    def _():
        kv[0, y, core] = part

    @pl.when(x_lo == 1)
    def _():
        kv[1, y, core] = part

    pl.semaphore_wait(barrier, 2 * REACH + 8)

    def a_copy(src, dst, d, xt):
        return push(
            kv.at[src, y, core], kv.at[dst, y, core], a_send.at[dst, xt], a_recv.at[dst],
            (lax.rem(ctx + d, n_ctx), xt * 8 + lax.rem(head, 8)),
        )

    first_sends = [(0, 0, 0, 1)] + [(0, 2 + d, d, xt) for d in (4, 3, 1, 2) for xt in range(2)]
    second_sends = [(1, 1, 0, 0)] + [(1, 2, 1, xt) for xt in range(2)]

    @pl.when(x_lo == 0)
    def _():
        for args in first_sends:
            a_copy(*args).start()

    @pl.when(x_lo == 1)
    def _():
        for args in second_sends:
            a_copy(*args).start()

    def project(ks):
        total = None
        for k in ks:
            qw_loads[k].wait()
            term = jnp.dot(
                hidden[:, k * deep : (k + 1) * deep], qw[k * deep : (k + 1) * deep, :],
                preferred_element_type=jnp.float32,
            )
            total = term if total is None else total + term
        return total

    groups = (slice(0, 2), slice(2, 5), slice(5, 7))

    def b_copy(g, k):
        piece = kv.at[groups[g], y, core]
        return push(
            piece, piece, b_send.at[g], b_recv.at[g],
            (ctx, x_lo * 8 + lax.rem(y + k, 4) * 2 + core),
        )

    def c_copy(g):
        piece = kv.at[groups[g], :, core]
        return push(piece, piece, c_send.at[g], c_recv.at[g], (ctx, sibling))

    def b_all(g):
        piece = kv.at[groups[g], 0:3, core]
        return push(piece, piece, b_send.at[g], b_recv.at[g], (ctx, sibling))

    def spread(g):
        for k in (2, 1, 3):
            b_copy(g, k).start()

    def forward(g):
        b_all(g).wait_recv()
        c_copy(g).start()

    def second(place, which):
        return kv[place, 2 * which : 2 * which + 2].astype(jnp.float32).reshape(HD, tokens)

    sa[0, 0:tokens, 0 : heads * HD] = project((0,))

    @pl.when(x_lo == 1)
    def _():
        a_copy(0, 0, 0, 0).wait_recv()

    @pl.when(x_lo == 0)
    def _():
        a_copy(0, 1, 0, 0).wait_recv()

    spread(0)
    sa[0, 0:tokens, 0 : heads * HD] = sa[0, 0:tokens, 0 : heads * HD] + project((1,))
    for place in (2, 3, 4):
        a_copy(0, place, 0, 0).wait_recv()
    spread(1)
    for place in (5, 6):
        a_copy(0, place, 0, 0).wait_recv()
    spread(2)
    forward(0)
    qs[...] = (sa[0, 0:tokens, 0 : heads * HD] + project((2, 3))).astype(jnp.bfloat16)
    forward(1)
    forward(2)
    c_copy(0).wait_recv()
    c_copy(1).wait_recv()

    t_iota = lax.broadcasted_iota(jnp.int32, (tokens, HD), 0)
    for which, dst in ((0, k2s), (1, v2s)):
        k2e[0:W2] = second(2, which).T[tokens - W2 :]
        k2e[W2 : W2 + tokens] = second(1, which).T
        for r in range(W2):
            moved = k2e[W2 - r : W2 - r + tokens]
            if r:
                other = k2e[W2 : W2 + tokens] if which == 0 else jnp.zeros_like(moved)
                moved = jnp.where((ctx > 0) | (t_iota >= r), moved, other)
            dst[r] = moved.astype(jnp.bfloat16)

    own_key = second(0, 0)
    blank = jnp.zeros((HD, HD), jnp.bfloat16)

    def pair_up(dst, block):
        dst[0:HD, 0:HD] = block
        dst[0:HD, HD : 2 * HD] = blank
        dst[HD : 2 * HD, 0:HD] = blank
        dst[HD : 2 * HD, HD : 2 * HD] = block

    for d in range(REACH + 1):
        if d == 3:
            c_copy(2).wait_recv()
        place = d + 2 if d else 0
        key = second(place, 0)
        value = second(place, 1).T
        ones = jnp.ones((HD, HD), jnp.float32)
        if d:
            here = ctx >= d
            key = jnp.where(here, key, own_key[:, 0:1]) * SCALE
            value = jnp.where(here, value, 0.0)
            ones = jnp.where(here, ones, 0.0)
            cols = slice((REACH - d) * HD, (REACH - d + 1) * HD)
            high = key.astype(jnp.bfloat16)
            keys[0:HD, cols] = high
            keys[HD : 2 * HD, cols] = (key - high.astype(jnp.float32)).astype(jnp.bfloat16)
        else:
            pair_up(keys_new, key.astype(jnp.bfloat16))
        if d == 1:
            pair_up(values_last, value.astype(jnp.bfloat16))
        else:
            first = {4: 0, 0: 1, 3: 2, 2: 3}[d] * HD
            values[first : first + HD, 0:HD] = value.astype(jnp.bfloat16)
            values[first : first + HD, HD : 2 * HD] = ones.astype(jnp.bfloat16)

    for item in loads[2:]:
        item.wait()

    n = W2 * TB

    def scores(pair, t0, buf, buf_new):
        k2 = k2s[:, pl.ds(t0, TB), :]
        mixed = []
        for j in range(2):
            h = pair * 2 + j
            q = qs[pl.ds(t0, TB), h * HD : (h + 1) * HD]
            mixed.append((k2 * q[None]).reshape(n, HD))
        for j in range(2):
            buf[j] = jnp.dot(
                jnp.concatenate([mixed[j], mixed[j]], axis=1), keys[...], preferred_element_type=jnp.float32
            )
        buf_new[...] = jnp.dot(
            jnp.concatenate(mixed, axis=1), keys_new[...], preferred_element_type=jnp.float32
        )

    def attend(pair, t0, buf, buf_new):
        tok = t0 + lax.broadcasted_iota(jnp.int32, (TB, HD), 0)
        col = lax.broadcasted_iota(jnp.int32, (TB, HD), 1)
        new = (col <= tok)[None]
        new_rows = jnp.broadcast_to(new, (W2, TB, HD)).reshape(n, HD)
        outs, last, last_sums = [], [], []
        for j in range(2):
            s = buf[j].reshape(W2, TB, 4 * HD)
            s_new = buf_new[:, j * HD : (j + 1) * HD].reshape(W2, TB, HD) * SCALE
            both = jnp.where(new, s_new, s[:, :, :HD])
            peak = jnp.maximum(
                jnp.maximum(both, s[:, :, HD : 2 * HD]),
                jnp.maximum(s[:, :, 2 * HD : 3 * HD], s[:, :, 3 * HD :]),
            )
            peak = jnp.max(jnp.max(peak, axis=0), axis=1, keepdims=True)[None]
            w_both = jnp.exp2(both - peak).astype(jnp.bfloat16).reshape(n, HD)
            w_old = jnp.where(new_rows, 0, w_both)
            w_new = jnp.where(new_rows, w_both, 0)
            w_mid = jnp.exp2(s[:, :, HD : 3 * HD] - peak).astype(jnp.bfloat16).reshape(n, 2 * HD)
            w_last = jnp.exp2(s[:, :, 3 * HD :] - peak)
            last_sums.append(jnp.sum(jnp.sum(w_last, axis=0), axis=1, keepdims=True))
            last.append(w_last.astype(jnp.bfloat16).reshape(n, HD))
            outs.append(
                jnp.dot(
                    jnp.concatenate([w_old, w_new, w_mid], axis=1), values[...],
                    preferred_element_type=jnp.float32,
                )
            )
        out_last = jnp.dot(
            jnp.concatenate(last, axis=1), values_last[...], preferred_element_type=jnp.float32
        )
        v2 = v2s[:, pl.ds(t0, TB), :].astype(jnp.float32)
        missing = jnp.where(ctx > 0, 0, jnp.maximum(W2 - 1 - tok, 0)).astype(jnp.float32)
        for j in range(2):
            h = pair * 2 + j
            o = outs[j].reshape(W2, TB, 2 * HD)
            o_last = out_last[:, j * HD : (j + 1) * HD].reshape(W2, TB, HD)
            num = jnp.sum((o[:, :, :HD] + o_last) * v2, axis=0)
            den = jnp.sum(o[:, :, HD:], axis=0) - missing * o[0, :, HD:]
            den = den + jnp.where(ctx > 0, last_sums[j], 0.0)
            att[pl.ds(t0, TB), h * HD : (h + 1) * HD] = (num / den).astype(jnp.bfloat16)

    scores(0, 0, sa, na)

    def r1_copy(b):
        return push(psib.at[b], r1.at[b], r1_send.at[b], r1_recv.at[b], (ctx, sibling))

    def r2_copy(b, k):
        to = lax.rem(chip + k, 8)
        return push(
            r2s.at[b, to], r2.at[b, k - 1], r2_send.at[b], r2_recv.at[b], (ctx, to * 2 + core)
        )

    def rows_of(b):
        return pl.ds(pl.multiple_of(b * T, T), T)

    def ag_copy(b, k):
        to = lax.rem(chip + k, 8)
        piece = ro.at[core, chip, rows_of(b)]
        return push(piece, piece, ag_send.at[b], ag_recv.at[b], (ctx, to * 2 + core))

    def r2_all(b):
        return push(r2s.at[b, 0:7], r2.at[b], r2_send.at[b], r2_recv.at[b], (ctx, sibling))

    def ag_all(b):
        pieces = ro.at[core, 0:7, rows_of(b)]
        return push(pieces, pieces, ag_send.at[b], ag_recv.at[b], (ctx, sibling))

    def sh_copy(b):
        piece = ro.at[core, :, rows_of(b)]
        return push(piece, piece, sh_send.at[b], sh_recv.at[b], (ctx, sibling))

    def out_copy(b):
        return pltpu.make_async_copy(ro.at[:, :, rows_of(b)], ro_hbm.at[:, :, rows_of(b)], out_sem.at[b])

    def product(b, to, to_core):
        cols = pl.ds(pl.multiple_of((to * 2 + to_core) * chunk, chunk), chunk)
        p = jnp.dot(att[rows_of(b), :], ow[:, cols], preferred_element_type=jnp.float32)
        row = lax.broadcasted_iota(jnp.int32, (T, chunk), 0) + (b * T - 8 * head)
        res = residual[:, cols].astype(jnp.float32)
        return p + jnp.where((row >= 0) & (row < 8), jnp.concatenate([res] * (T // 8), axis=0), 0.0)

    def event_project(b):
        for to in range(8):
            psib[b, to] = product(b, to, 1 - core).astype(jnp.bfloat16)
        r1_copy(b).start()
        for to in range(8):
            pown[b, to] = product(b, to, core)

    def event_scatter(b):
        r1_copy(b).wait_recv()
        for k in (6, 2, 5, 3, 7, 1, 4):
            to = lax.rem(chip + k, 8)
            r2s[b, to] = (pown[b, to] + r1[b, to].astype(jnp.float32)).astype(jnp.bfloat16)
            r2_copy(b, k).start()

    def event_reduce(b):
        total = pown[b, chip] + r1[b, chip].astype(jnp.float32)
        r2_all(b).wait_recv()
        for k in range(1, 8):
            total = total + r2[b, k - 1].astype(jnp.float32)
        ro[core, chip, rows_of(b), :] = total.astype(jnp.bfloat16)
        for k in (6, 2, 5, 3, 7, 1, 4):
            ag_copy(b, k).start()

    def event_share(b):
        ag_all(b).wait_recv()
        sh_copy(b).start()

    def event_leave(b):
        piece = ro.at[1 - core, :, rows_of(b)]
        push(piece, piece, sh_send.at[b], sh_recv.at[b], (ctx, sibling)).wait_recv()
        out_copy(b).start()

    per = T // TB

    def finish(b, _):
        r1_copy(b).wait_send()
        r2_all(b).wait_send()
        ag_all(b).wait_send()
        sh_copy(b).wait_send()
        out_copy(b).wait()
        return 0

    def settle():
        @pl.when(x_lo == 0)
        def _():
            for args in first_sends:
                a_copy(*args).wait_send()

        @pl.when(x_lo == 1)
        def _():
            for args in second_sends:
                a_copy(*args).wait_send()

        for g in range(3):
            b_all(g).wait_send()
            c_copy(g).wait_send()

    def step(i, _):
        @pl.when(i < steps)
        def _():
            t0 = pl.multiple_of(i * TB, TB)
            later = pl.multiple_of(jnp.minimum(i + 1, steps - 1) * TB, TB)
            scores(1, t0, sb, nb)
            attend(0, t0, sa, na)
            scores(0, later, sa, na)
            attend(1, t0, sb, nb)

        def at(lag, event):
            j = i + 1 - lag
            b = j // per

            @pl.when((j >= per) & (lax.rem(j, per) == 0) & (b <= n_blocks))
            def _():
                event(b - 1)

        @pl.when(i == steps + LAGS[0])
        def _():
            settle()

        at(LAGS[3], event_leave)
        at(LAGS[2], event_share)
        at(LAGS[1], event_reduce)
        at(LAGS[0], event_scatter)
        at(0, event_project)
        return 0

    lax.fori_loop(0, steps + LAGS[3], step, 0)

    lax.fori_loop(0, n_blocks, finish, 0)


def norm_kernel(ro, gain, rout_ref, normed_ref):
    head = lax.axis_index("head")
    tokens, width = normed_ref.shape
    chunk = width // 16
    square = jnp.zeros((tokens, chunk), jnp.float32)
    for c in range(2):
        for to in range(8):
            v = ro[c, to].astype(jnp.float32)
            square = square + v * v
    scale = lax.rsqrt(jnp.sum(square, axis=1, keepdims=True) * (1.0 / width) + 1e-05)
    for c in range(2):
        for to in range(8):
            cols = slice((to * 2 + c) * chunk, (to * 2 + c + 1) * chunk)
            normed_ref[:, cols] = (ro[c, to].astype(jnp.float32) * scale * gain[:, cols]).astype(jnp.bfloat16)
            v = ro[c, to, pl.ds(pl.multiple_of(head // 2 * 16, 16), 16), :].astype(jnp.float32)
            rout_ref[:, cols] = jnp.where(lax.rem(head, 2) == 0, v[:8], v[8:]).astype(jnp.bfloat16)


def body(hidden_in, query_weight, shared_weight, out_weight, residual, norm_gain):
    tokens, width = hidden_in.shape
    columns = query_weight.shape[1]
    blocks = tokens // T
    chunk = width // 16
    vmem = lambda shape, dtype=jnp.bfloat16: pltpu.VMEM(shape, dtype)
    dma = lambda *shape: pltpu.SemaphoreType.DMA(shape)
    anywhere = pl.BlockSpec(memory_space=pl.ANY)
    rows = W2 * TB
    whole = pl.BlockSpec(memory_space=pltpu.VMEM)
    gathered = pl.pallas_call(
        kernel,
        out_shape=jax.ShapeDtypeStruct((2, 8, tokens, chunk), jnp.bfloat16),
        in_specs=[anywhere] * 5,
        out_specs=anywhere,
        scratch_shapes=[
            vmem((tokens, width)),
            vmem((width, columns)),
            vmem(shared_weight.shape[::-1]),
            vmem(out_weight.shape),
            vmem(residual.shape),
            vmem((REACH + 3, 4, 2, 32, tokens)),
            vmem((2 * HD, REACH * HD)),
            vmem((2 * HD, 2 * HD)),
            vmem((REACH * HD, 2 * HD)),
            vmem((2 * HD, 2 * HD)),
            vmem((W2 + tokens, HD), jnp.float32),
            vmem((W2, tokens, HD)),
            vmem((W2, tokens, HD)),
            vmem((tokens, columns)),
            vmem((tokens, columns)),
            vmem((2, rows, REACH * HD), jnp.float32),
            vmem((rows, 2 * HD), jnp.float32),
            vmem((2, rows, REACH * HD), jnp.float32),
            vmem((rows, 2 * HD), jnp.float32),
            vmem((blocks, 8, T, chunk)),
            vmem((blocks, 8, T, chunk), jnp.float32),
            vmem((blocks, 8, T, chunk)),
            vmem((blocks, 8, T, chunk)),
            vmem((blocks, 7, T, chunk)),
            vmem((2, 8, tokens, chunk)),
            dma(4), dma(4), dma(blocks),
            dma(REACH + 3, 2), dma(REACH + 3),
            dma(3), dma(3),
            dma(3), dma(3),
            dma(blocks), dma(blocks),
            dma(blocks), dma(blocks),
            dma(blocks), dma(blocks),
            dma(blocks), dma(blocks),
        ],
        compiler_params=pltpu.CompilerParams(
            collective_id=0, has_side_effects=True, vmem_limit_bytes=56 * 2**20
        ),
    )(hidden_in, query_weight, shared_weight.T, out_weight, residual)
    return tuple(
        pl.pallas_call(
            norm_kernel,
            out_shape=(
                jax.ShapeDtypeStruct(residual.shape, jnp.bfloat16),
                jax.ShapeDtypeStruct(hidden_in.shape, jnp.bfloat16),
            ),
            in_specs=[whole] * 2,
            out_specs=(whole, whole),
        )(gathered, norm_gain.reshape(1, width))
    )


def solution(mesh):
    in_specs = (
        P("ctx", None),
        P(None, "head"),
        P(None, "head"),
        P("head", None),
        P(("ctx", "head"), None),
        P(),
    )
    out_specs = (P(("ctx", "head"), None), P("ctx", None))
    return jax.shard_map(body, mesh=mesh, in_specs=in_specs, out_specs=out_specs, check_vma=False)
```

time: 77.6 us -> 55.9 us (0.72)
  Pallas kernels: 70.7 us -> 55.1 us
  local copies, waits for them, and re-layouts: 6.03 us -> 0 us
    pallas_call x1 -> x2, Pallas kernels: 70.7 us -> 55.1 us  [the longest x1 52.4 us: body(): pl.pallas_call(kernel, out_shape=jax.ShapeDtypeStruct((2, 8, tokens, chun...]
    unnamed x3 -> x0, local copies, waits for them, and re-layouts: 6.03 us -> none
where the time goes in v2:
time: 55.9 us; the launch traced here: 55.7 us
  Pallas kernels  55.1 us (99%)
  between operations  0.64 us (1%)
    pallas_call x1, Pallas kernels, body(): pl.pallas_call(kernel, out_shape=jax.ShapeDtypeStruct((2, 8, tokens, chun...  52.4 us
    pallas_call x1, Pallas kernels, body(): pl.pallas_call(norm_kernel, out_shape=(jax.ShapeDtypeStruct(residual.shap...  2.66 us

profile of v2, /device:TPU:1, one launch (start us, length us, event | category | flops | bytes accessed | tf_op | source)
XLA Modules:
  0.0 55.7 jit_solution(5610867846171142492)
XLA Ops:
  0.6 52.4 %shard_map.77.ro = bf16[2,8,128,256]{3,2,1,0:T(8,128)(2,1)} custom-call(bf16[128,4096]{1,0:T(8,128)(2,1)} %hidden_hbm.1, bf16[4096,512]{1,0:T(8,128)(2,1)} %qw_hbm.1, bf16[32,4096]{1,0:T(8,128)(2,1)} %bitcast.2, bf16[512,4096]{1,0:T(8,128)(2,1)} %ow_hbm.1, bf16[8,4096]{1,0:T(8,128)(2,1)} %residual_hbm.1), custom_call_target="tpu_custom_call" | custom-call | tf_op jit(solution)/shard_map/pallas_call | solution.py:454
  53.1 2.7 %shard_map.78 = (bf16[8,4096]{1,0:T(8,128)(2,1)}, bf16[128,4096]{1,0:T(8,128)(2,1)}) custom-call(bf16[2,8,128,256]{3,2,1,0:T(8,128)(2,1)} %shard_map.77.ro, f32[1,4096]{1,0:T(1,128)} %bitcast.3), custom_call_target="tpu_custom_call" | custom-call | tf_op jit(solution)/shard_map/pallas_call | solution.py:499

commit v3 on v2

--- a/solution.py
+++ b/solution.py
@@ -108,7 +108,8 @@
             (lax.rem(ctx + d, n_ctx), xt * 8 + lax.rem(head, 8)),
         )
 
-    first_sends = [(0, 0, 0, 1)] + [(0, 2 + d, d, xt) for d in (4, 3, 1, 2) for xt in range(2)]
+    first_sends = [(0, 2 + d, d, xt) for d in (4, 3) for xt in range(2)] + [(0, 0, 0, 1)]
+    first_sends += [(0, 2 + d, d, xt) for d in (1, 2) for xt in range(2)]
     second_sends = [(1, 1, 0, 0)] + [(1, 2, 1, xt) for xt in range(2)]
 
     @pl.when(x_lo == 0)
@@ -132,7 +133,7 @@
             total = term if total is None else total + term
         return total
 
-    groups = (slice(0, 2), slice(2, 5), slice(5, 7))
+    groups = (slice(0, 4), slice(4, 7))
 
     def b_copy(g, k):
         piece = kv.at[groups[g], y, core]
@@ -160,7 +161,7 @@
     def second(place, which):
         return kv[place, 2 * which : 2 * which + 2].astype(jnp.float32).reshape(HD, tokens)
 
-    sa[0, 0:tokens, 0 : heads * HD] = project((0,))
+    sa[0, 0:tokens, 0 : heads * HD] = project((0, 1))
 
     @pl.when(x_lo == 1)
     def _():
@@ -170,20 +171,15 @@
     def _():
         a_copy(0, 1, 0, 0).wait_recv()
 
+    for place in (2, 3):
+        a_copy(0, place, 0, 0).wait_recv()
     spread(0)
-    sa[0, 0:tokens, 0 : heads * HD] = sa[0, 0:tokens, 0 : heads * HD] + project((1,))
-    for place in (2, 3, 4):
+    qs[...] = (sa[0, 0:tokens, 0 : heads * HD] + project((2, 3))).astype(jnp.bfloat16)
+    for place in (4, 5, 6):
         a_copy(0, place, 0, 0).wait_recv()
     spread(1)
-    for place in (5, 6):
-        a_copy(0, place, 0, 0).wait_recv()
-    spread(2)
     forward(0)
-    qs[...] = (sa[0, 0:tokens, 0 : heads * HD] + project((2, 3))).astype(jnp.bfloat16)
-    forward(1)
-    forward(2)
     c_copy(0).wait_recv()
-    c_copy(1).wait_recv()
 
     t_iota = lax.broadcasted_iota(jnp.int32, (tokens, HD), 0)
     for which, dst in ((0, k2s), (1, v2s)):
@@ -196,6 +192,8 @@
                 moved = jnp.where((ctx > 0) | (t_iota >= r), moved, other)
             dst[r] = moved.astype(jnp.bfloat16)
 
+    forward(1)
+
     own_key = second(0, 0)
     blank = jnp.zeros((HD, HD), jnp.bfloat16)
 
@@ -206,8 +204,8 @@
         dst[HD : 2 * HD, HD : 2 * HD] = block
 
     for d in range(REACH + 1):
-        if d == 3:
-            c_copy(2).wait_recv()
+        if d == 2:
+            c_copy(1).wait_recv()
         place = d + 2 if d else 0
         key = second(place, 0)
         value = second(place, 1).T
@@ -294,11 +292,14 @@
 
     scores(0, 0, sa, na)
 
+    def other(k):
+        return lax.rem(x_lo + k // 4, 2) * 4 + lax.rem(y + k % 4, 4)
+
     def r1_copy(b):
         return push(psib.at[b], r1.at[b], r1_send.at[b], r1_recv.at[b], (ctx, sibling))
 
     def r2_copy(b, k):
-        to = lax.rem(chip + k, 8)
+        to = other(k)
         return push(
             r2s.at[b, to], r2.at[b, k - 1], r2_send.at[b], r2_recv.at[b], (ctx, to * 2 + core)
         )
@@ -307,7 +308,7 @@
         return pl.ds(pl.multiple_of(b * T, T), T)
 
     def ag_copy(b, k):
-        to = lax.rem(chip + k, 8)
+        to = other(k)
         piece = ro.at[core, chip, rows_of(b)]
         return push(piece, piece, ag_send.at[b], ag_recv.at[b], (ctx, to * 2 + core))
 
@@ -341,8 +342,8 @@
 
     def event_scatter(b):
         r1_copy(b).wait_recv()
-        for k in (6, 2, 5, 3, 7, 1, 4):
-            to = lax.rem(chip + k, 8)
+        for k in (6, 2, 5, 7, 1, 3, 4):
+            to = other(k)
             r2s[b, to] = (pown[b, to] + r1[b, to].astype(jnp.float32)).astype(jnp.bfloat16)
             r2_copy(b, k).start()
 
@@ -352,7 +353,7 @@
         for k in range(1, 8):
             total = total + r2[b, k - 1].astype(jnp.float32)
         ro[core, chip, rows_of(b), :] = total.astype(jnp.bfloat16)
-        for k in (6, 2, 5, 3, 7, 1, 4):
+        for k in (6, 2, 5, 7, 1, 3, 4):
             ag_copy(b, k).start()
 
     def event_share(b):
@@ -385,7 +386,7 @@
             for args in second_sends:
                 a_copy(*args).wait_send()
 
-        for g in range(3):
+        for g in range(2):
             b_all(g).wait_send()
             c_copy(g).wait_send()
 
@@ -425,9 +426,9 @@
 
 def norm_kernel(ro, gain, rout_ref, normed_ref):
     head = lax.axis_index("head")
-    tokens, width = normed_ref.shape
+    some, width = normed_ref.shape
     chunk = width // 16
-    square = jnp.zeros((tokens, chunk), jnp.float32)
+    square = jnp.zeros((some, chunk), jnp.float32)
     for c in range(2):
         for to in range(8):
             v = ro[c, to].astype(jnp.float32)
@@ -437,8 +438,17 @@
         for to in range(8):
             cols = slice((to * 2 + c) * chunk, (to * 2 + c + 1) * chunk)
             normed_ref[:, cols] = (ro[c, to].astype(jnp.float32) * scale * gain[:, cols]).astype(jnp.bfloat16)
-            v = ro[c, to, pl.ds(pl.multiple_of(head // 2 * 16, 16), 16), :].astype(jnp.float32)
-            rout_ref[:, cols] = jnp.where(lax.rem(head, 2) == 0, v[:8], v[8:]).astype(jnp.bfloat16)
+
+    per = some // 8
+
+    @pl.when(pl.program_id(0) == head // per)
+    def _():
+        row = pl.multiple_of(lax.rem(head, per) // 2 * 16, 16)
+        for c in range(2):
+            for to in range(8):
+                cols = slice((to * 2 + c) * chunk, (to * 2 + c + 1) * chunk)
+                v = ro[c, to, pl.ds(row, 16), :].astype(jnp.float32)
+                rout_ref[:, cols] = jnp.where(lax.rem(head, 2) == 0, v[:8], v[8:]).astype(jnp.bfloat16)
 
 
 def body(hidden_in, query_weight, shared_weight, out_weight, residual, norm_gain):
@@ -484,8 +494,8 @@
             vmem((2, 8, tokens, chunk)),
             dma(4), dma(4), dma(blocks),
             dma(REACH + 3, 2), dma(REACH + 3),
-            dma(3), dma(3),
-            dma(3), dma(3),
+            dma(2), dma(2),
+            dma(2), dma(2),
             dma(blocks), dma(blocks),
             dma(blocks), dma(blocks),
             dma(blocks), dma(blocks),
@@ -502,8 +512,15 @@
                 jax.ShapeDtypeStruct(residual.shape, jnp.bfloat16),
                 jax.ShapeDtypeStruct(hidden_in.shape, jnp.bfloat16),
             ),
-            in_specs=[whole] * 2,
-            out_specs=(whole, whole),
+            grid=(2,),
+            in_specs=[
+                pl.BlockSpec((2, 8, tokens // 2, chunk), lambda i: (0, 0, i, 0)),
+                pl.BlockSpec((1, width), lambda i: (0, 0)),
+            ],
+            out_specs=(
+                pl.BlockSpec(residual.shape, lambda i: (0, 0)),
+                pl.BlockSpec((tokens // 2, width), lambda i: (i, 0)),
+            ),
         )(gathered, norm_gain.reshape(1, width))
     )
 

time: 55.9 us -> 55.2 us (0.987)
  Pallas kernels: 55.1 us -> 54.5 us
where the time goes in v3:
time: 55.2 us; the launch traced here: 55.1 us
  Pallas kernels  54.5 us (99%)
  between operations  0.64 us (1%)
    pallas_call x1, Pallas kernels, body(): pl.pallas_call(kernel, out_shape=jax.ShapeDtypeStruct((2, 8, tokens, chun...  52.1 us
    pallas_call x1, Pallas kernels, body(): pl.pallas_call(norm_kernel, out_shape=(jax.ShapeDtypeStruct(residual.shap...  2.38 us

profile of v3, /device:TPU:1, one launch (start us, length us, event | category | flops | bytes accessed | tf_op | source)
XLA Modules:
  0.0 55.1 jit_solution(8839284764283356619)
XLA Ops:
  0.6 52.1 %shard_map.77.ro = bf16[2,8,128,256]{3,2,1,0:T(8,128)(2,1)} custom-call(bf16[128,4096]{1,0:T(8,128)(2,1)} %hidden_hbm.1, bf16[4096,512]{1,0:T(8,128)(2,1)} %qw_hbm.1, bf16[32,4096]{1,0:T(8,128)(2,1)} %bitcast.2, bf16[512,4096]{1,0:T(8,128)(2,1)} %ow_hbm.1, bf16[8,4096]{1,0:T(8,128)(2,1)} %residual_hbm.1), custom_call_target="tpu_custom_call" | custom-call | tf_op jit(solution)/shard_map/pallas_call | solution.py:464
  52.7 2.4 %shard_map.78 = (bf16[8,4096]{1,0:T(8,128)(2,1)}, bf16[128,4096]{1,0:T(8,128)(2,1)}) custom-call(bf16[2,8,128,256]{3,2,1,0:T(8,128)(2,1)} %shard_map.77.ro, f32[1,4096]{1,0:T(1,128)} %bitcast.3), custom_call_target="tpu_custom_call" | custom-call | tf_op jit(solution)/shard_map/pallas_call | solution.py:509

commit v4 on v3

--- a/solution.py
+++ b/solution.py
@@ -14,7 +14,7 @@
 TB = 16
 T = 32
 REACH = 4
-LAGS = (1, 4, 7, 8)
+LAGS = (1, 3, 5, 6)
 MESH = pl.DeviceIdType.MESH
 SCALE = HD**-0.5 * math.log2(math.e)
 
@@ -39,7 +39,6 @@
     tokens, width = hidden_hbm.shape
     heads = qw_hbm.shape[1] // HD
     n_blocks = tokens // T
-    steps = tokens // TB
     chunk = width // 16
     sibling = chip * 2 + 1 - core
 
@@ -391,35 +390,34 @@
             c_copy(g).wait_send()
 
     def step(i, _):
-        @pl.when(i < steps)
+        @pl.when(i < n_blocks)
         def _():
-            t0 = pl.multiple_of(i * TB, TB)
-            later = pl.multiple_of(jnp.minimum(i + 1, steps - 1) * TB, TB)
-            scores(1, t0, sb, nb)
-            attend(0, t0, sa, na)
-            scores(0, later, sa, na)
-            attend(1, t0, sb, nb)
+            for u in range(per):
+                t0 = pl.multiple_of(i * T + u * TB, TB)
+                later = pl.multiple_of(jnp.minimum(i * T + (u + 1) * TB, tokens - TB), TB)
+                scores(1, t0, sb, nb)
+                attend(0, t0, sa, na)
+                scores(0, later, sa, na)
+                attend(1, t0, sb, nb)
 
         def at(lag, event):
-            j = i + 1 - lag
-            b = j // per
-
-            @pl.when((j >= per) & (lax.rem(j, per) == 0) & (b <= n_blocks))
+            @pl.when((i >= lag) & (i - lag < n_blocks))
             def _():
-                event(b - 1)
-
-        @pl.when(i == steps + LAGS[0])
+                event(i - lag)
+
+        at(LAGS[0], event_scatter)
+        at(0, event_project)
+        at(LAGS[1], event_reduce)
+
+        @pl.when(i == n_blocks)
         def _():
             settle()
 
+        at(LAGS[2], event_share)
         at(LAGS[3], event_leave)
-        at(LAGS[2], event_share)
-        at(LAGS[1], event_reduce)
-        at(LAGS[0], event_scatter)
-        at(0, event_project)
         return 0
 
-    lax.fori_loop(0, steps + LAGS[3], step, 0)
+    lax.fori_loop(0, n_blocks + LAGS[3], step, 0)
 
     lax.fori_loop(0, n_blocks, finish, 0)
 

time: 55.2 us -> 55.1 us (level)
  no operation moved by 1% of the time
where the time goes in v4:
time: 55.1 us; the launch traced here: 55 us
  Pallas kernels  54.3 us (99%)
  between operations  0.64 us (1%)
    pallas_call x1, Pallas kernels, body(): pl.pallas_call(kernel, out_shape=jax.ShapeDtypeStruct((2, 8, tokens, chun...  51.9 us
    pallas_call x1, Pallas kernels, body(): pl.pallas_call(norm_kernel, out_shape=(jax.ShapeDtypeStruct(residual.shap...  2.38 us

profile of v4, /device:TPU:1, one launch (start us, length us, event | category | flops | bytes accessed | tf_op | source)
XLA Modules:
  0.0 55.0 jit_solution(10336157323103955520)
XLA Ops:
  0.6 51.9 %shard_map.77.ro = bf16[2,8,128,256]{3,2,1,0:T(8,128)(2,1)} custom-call(bf16[128,4096]{1,0:T(8,128)(2,1)} %hidden_hbm.1, bf16[4096,512]{1,0:T(8,128)(2,1)} %qw_hbm.1, bf16[32,4096]{1,0:T(8,128)(2,1)} %bitcast.2, bf16[512,4096]{1,0:T(8,128)(2,1)} %ow_hbm.1, bf16[8,4096]{1,0:T(8,128)(2,1)} %residual_hbm.1), custom_call_target="tpu_custom_call" | custom-call | tf_op jit(solution)/shard_map/pallas_call | solution.py:462
  52.6 2.4 %shard_map.78 = (bf16[8,4096]{1,0:T(8,128)(2,1)}, bf16[128,4096]{1,0:T(8,128)(2,1)}) custom-call(bf16[2,8,128,256]{3,2,1,0:T(8,128)(2,1)} %shard_map.77.ro, f32[1,4096]{1,0:T(1,128)} %bitcast.3), custom_call_target="tpu_custom_call" | custom-call | tf_op jit(solution)/shard_map/pallas_call | solution.py:507
